TPU v7x, 32 devices: a whole 2x2x4 slice. The times are simulated.
32 devices in a mesh: groups: 2 (over x), pool: 1, tensor: 16 (over z, y, core).
Axes of the slice: x: 2, y: 2, z: 4, core: 2. Of those that a mesh axis runs over, the one named last changes fastest.
Arguments:
- hidden_state: bfloat16 [128, 8192], P(('groups', 'pool', 'tensor')), parts along dimension 0, may hold values from -6 to 6
- query_weight: bfloat16 [8192, 8192], P(None, 'tensor'), may hold values from -0.0625 to 0.0625
- keyval_weight: bfloat16 [8192, 2048], P(None, 'tensor'), may hold values from -0.0625 to 0.0625
- output_weight: bfloat16 [8192, 8192], P('tensor'), may hold values from -0.0625 to 0.0625
- cache_entries: bfloat16 [128, 48, 8, 256], P(('groups', 'pool', 'tensor')), parts along dimension 0, may hold values from -256 to 256
- adapter_pool: bfloat16 [64, 4, 16, 8192], P(('groups', 'pool', 'tensor')), parts along dimension 0, may hold values from -3 to 3
- page_table: int32 [64], P('groups'), parts along dimension 0, may hold values from 0 to 31, as said below
- fetch_list: int32 [64], P('groups'), parts along dimension 0, may hold values from 0 to 31, as said below
- row_tenant: int32 [128], P(('groups', 'pool')), parts along dimension 0, may hold values from 0 to 31, as said below
- cache_length: int32 [128], P(('groups', 'pool', 'tensor')), parts along dimension 0, may hold values from 1 to 46, as said below
Outputs:
- updates: bfloat16 [2, 128, 8192], P(None, ('groups', 'pool', 'tensor')), parts along dimension 1
There are 2 independent parts, one for each index of `groups`. A program takes and returns all parts, laid end to end along the dimension named above; an argument that names none is the same for every part. Nothing has to cross between parts.
Inputs may be any that keep to these rules, and one draw needn't show every extreme that they name: `fetch_list`: 32 different tenants. `page_table`: a one-to-one map of tenants to pages; page p lies on the device of index p // 2 over pool and tensor (pool index major), in its local slot p % 2; no device holds the pages of more than 2 fetched tenants, and some device holds exactly 2. `row_tenant`: every row's tenant is in fetch_list; in the rows of each index of pool every fetched tenant has some row. `cache_length`: some row has exactly 46.
All inputs are finite; a program needn't handle non-finite values.
Results may differ from a plain program's by a relative error of at most 0.035.
Values may be sent and summed in bfloat16 or wider, within the bound.
A program may use at most 128 MiB of HBM per device.

v0:
```python
import jax
import jax.numpy as jnp
from jax import lax
from jax.sharding import PartitionSpec as P

HEADS = 64
KVH = 8
HD = 128
FETCH = 32


rope_base = 500000.0
norm_epsilon = 1e-05


def rotate(vectors, positions):
    half_dim = vectors.shape[-1] // 2
    frequency = rope_base ** (-2.0 * jnp.arange(half_dim, dtype=jnp.float32) / vectors.shape[-1])
    angles = positions.astype(jnp.float32)[:, None] * frequency[None, :]
    cosine_term = jnp.cos(angles)[:, None, :]
    sine_term = jnp.sin(angles)[:, None, :]
    lead_half = vectors[..., :half_dim]
    trail_half = vectors[..., half_dim:]
    return jnp.concatenate(
        [
            lead_half * cosine_term - trail_half * sine_term,
            trail_half * cosine_term + lead_half * sine_term,
        ],
        axis=-1,
    )


def attend(query_rot, new_keys, new_values, cache_entries, cache_length):
    row_total = query_rot.shape[0]
    key_heads = cache_entries.shape[2]
    head_dim = query_rot.shape[2]
    group_size = query_rot.shape[1] // key_heads
    query_vectors = query_rot.reshape(row_total, key_heads, group_size, head_dim)
    cached_keys = cache_entries[..., :head_dim]
    cached_values = cache_entries[..., head_dim:]
    scale = float(head_dim) ** (-0.5)
    scores_cache = (
        jnp.einsum(
            "rhgd,rchd->rhgc", query_vectors, cached_keys, preferred_element_type=jnp.float32
        )
        * scale
    )
    in_length = jnp.arange(cache_entries.shape[1], dtype=jnp.int32)[None, :] < cache_length[:, None]
    scores_cache = jnp.where(in_length[:, None, None, :], scores_cache, -1e30)
    scores_new = (
        jnp.einsum("rhgd,rjhd->rhgj", query_vectors, new_keys, preferred_element_type=jnp.float32)
        * scale
    )
    highest = jnp.maximum(jnp.max(scores_cache, axis=-1), jnp.max(scores_new, axis=-1))[..., None]
    exp_cache = jnp.exp(scores_cache - highest)
    exp_new = jnp.exp(scores_new - highest)
    denominator = jnp.sum(exp_cache, axis=-1, keepdims=True) + jnp.sum(
        exp_new, axis=-1, keepdims=True
    )
    weight_cache = (exp_cache / denominator).astype(jnp.bfloat16)
    weight_new = (exp_new / denominator).astype(jnp.bfloat16)
    combined = jnp.einsum(
        "rhgc,rchd->rhgd", weight_cache, cached_values, preferred_element_type=jnp.float32
    )
    combined = combined + jnp.einsum(
        "rhgj,rjhd->rhgd", weight_new, new_values, preferred_element_type=jnp.float32
    )
    return combined.reshape(row_total, -1).astype(jnp.bfloat16)


def expand_matrix(shrink_matrix, selector_lowrank, up_adapter_tiles):
    spread = selector_lowrank[:, :, None] * shrink_matrix[:, None, :]
    return jnp.einsum("nfk,fkc->nc", spread, up_adapter_tiles, preferred_element_type=jnp.float32)


def on_device(
    hidden_state,
    query_weight,
    keyval_weight,
    output_weight,
    cache_entries,
    adapter_pool,
    page_table,
    fetch_list,
    row_tenant,
    cache_length,
):
    tensor_count = lax.axis_size("tensor")
    pool_count = lax.axis_size("pool")
    tensor_index = lax.axis_index("tensor")
    device_index = lax.axis_index("pool") * tensor_count + tensor_index
    row_count = hidden_state.shape[0]
    model_width = hidden_state.shape[1]
    block_width = model_width // tensor_count
    slot_count = adapter_pool.shape[0]
    owner_count = pool_count * tensor_count
    capacity = max(2, (FETCH + owner_count - 1) // owner_count)
    matched = fetch_list[:, None] == jnp.arange(page_table.shape[0], dtype=jnp.int32)[None, :]
    page_ids = jnp.sum(jnp.where(matched, page_table[None, :], 0), axis=1)
    owners = page_ids // slot_count
    slot_ids = page_ids % slot_count
    fetch_order = jnp.arange(FETCH, dtype=jnp.int32)
    earlier = (owners[:, None] == owners[None, :]) & (fetch_order[None, :] < fetch_order[:, None])
    owner_rank = jnp.sum(earlier.astype(jnp.int32), axis=1)
    owned_here = owners == device_index
    chosen = owned_here[None, :] & (
        owner_rank[None, :] == jnp.arange(capacity, dtype=jnp.int32)[:, None]
    )
    send_slots = jnp.sum(jnp.where(chosen, slot_ids[None, :], 0), axis=1)
    present = jnp.any(chosen, axis=1).astype(jnp.bfloat16)
    outgoing = jnp.take(adapter_pool, send_slots, axis=0) * present[:, None, None, None]
    doubled = jnp.concatenate([outgoing] * pool_count, axis=3)
    arrived = lax.all_to_all(doubled, ("pool", "tensor"), split_axis=3, concat_axis=0, tiled=True)
    adapter_tiles = jnp.take(arrived, owners * capacity + owner_rank, axis=0)
    down_query = adapter_tiles[:, 0]
    up_query = adapter_tiles[:, 1]
    down_out = adapter_tiles[:, 2]
    up_projected = adapter_tiles[:, 3]
    row_hits = row_tenant[:, None] == fetch_list[None, :]
    onehot_wide = row_hits.astype(jnp.float32)
    selector_lowrank = row_hits.astype(jnp.bfloat16)
    column_start = tensor_index * block_width
    query_cols = query_weight.shape[1]
    keyval_cols = keyval_weight.shape[1]
    residual = hidden_state
    new_keys = []
    new_values = []
    updates = []
    for step_index in range(2):
        widened = residual.astype(jnp.float32)
        normalized_input = (
            widened * lax.rsqrt(jnp.mean(widened * widened, axis=1, keepdims=True) + norm_epsilon)
        ).astype(jnp.bfloat16)
        features_part = lax.all_gather(normalized_input, "tensor", axis=0, tiled=True)
        query_baseline = jnp.dot(features_part, query_weight, preferred_element_type=jnp.float32)
        keyval = jnp.dot(features_part, keyval_weight, preferred_element_type=jnp.float32)
        own_cols = lax.dynamic_slice_in_dim(features_part, column_start, block_width, 1)
        per_tenant = jnp.einsum(
            "nd,fkd->nfk", own_cols, down_query, preferred_element_type=jnp.float32
        )
        shrink_matrix = jnp.sum(per_tenant * onehot_wide[:, :, None], axis=1)
        projected = jnp.concatenate([query_baseline, keyval, shrink_matrix], axis=1)
        shrink_query = lax.psum(projected[:, query_cols + keyval_cols :], "tensor").astype(
            jnp.bfloat16
        )
        query_vectors = (
            projected[:, :query_cols] + expand_matrix(shrink_query, selector_lowrank, up_query)
        ).astype(jnp.bfloat16)
        keyval = projected[:, query_cols : query_cols + keyval_cols].astype(jnp.bfloat16)
        query_rows, keyval_rows = (
            lax.all_to_all(query_vectors, "tensor", split_axis=0, concat_axis=1, tiled=True),
            lax.all_to_all(keyval, "tensor", split_axis=0, concat_axis=1, tiled=True),
        )
        positions = cache_length + step_index
        query_rot = rotate(
            query_rows.reshape(row_count, HEADS, HD).astype(jnp.float32), positions
        ).astype(jnp.bfloat16)
        keyval_rows = keyval_rows.reshape(row_count, KVH, 2 * HD)
        key_rot = rotate(keyval_rows[..., :HD].astype(jnp.float32), positions).astype(jnp.bfloat16)
        new_keys.append(key_rot)
        new_values.append(keyval_rows[..., HD:])
        attention_result = attend(
            query_rot,
            jnp.stack(new_keys, axis=1),
            jnp.stack(new_values, axis=1),
            cache_entries,
            cache_length,
        )
        head_rows = lax.all_to_all(
            attention_result, "tensor", split_axis=1, concat_axis=0, tiled=True
        )
        base_total = lax.psum_scatter(
            jnp.dot(head_rows, output_weight, preferred_element_type=jnp.float32),
            "tensor",
            scatter_dimension=0,
            tiled=True,
        )
        per_tenant = jnp.einsum(
            "nc,fkc->nfk", head_rows, down_out, preferred_element_type=jnp.float32
        )
        partial_out = jnp.sum(per_tenant * onehot_wide[:, :, None], axis=1)
        reduced_output = lax.psum(partial_out, "tensor").astype(jnp.bfloat16)
        adapter_columns = expand_matrix(reduced_output, selector_lowrank, up_projected)
        adapter_portion = lax.all_to_all(
            adapter_columns, "tensor", split_axis=0, concat_axis=1, tiled=True
        )
        state_update = (base_total + adapter_portion).astype(jnp.bfloat16)
        updates.append(state_update)
        residual = (residual.astype(jnp.float32) + state_update.astype(jnp.float32)).astype(
            jnp.bfloat16
        )
    return jnp.stack(updates)


def solution(mesh):
    return jax.shard_map(
        on_device,
        mesh=mesh,
        in_specs=(
            P(("groups", "pool", "tensor"), None),
            P(None, "tensor"),
            P(None, "tensor"),
            P("tensor", None),
            P(("groups", "pool", "tensor"), None, None, None),
            P(("groups", "pool", "tensor"), None, None, None),
            P("groups"),
            P("groups"),
            P(("groups", "pool")),
            P(("groups", "pool", "tensor")),
        ),
        out_specs=P(None, ("groups", "pool", "tensor"), None),
        check_vma=False,
    )
```

profile of v0, /device:TPU:0, one launch (start us, length us, event | category | flops | bytes accessed | tf_op | source)
XLA Modules:
  0.0 584.8 jit_solution(10220111437417458624)
XLA Ops:
  12.7 37.5 %all-gather.5.cloned.1.call-done = bf16[16,4,8192]{2,1,0:T(4,128)(2,1)} async-done(((bf16[1,4,8192]{2,1,0:T(4,128)(2,1)}), bf16[16,4,8192]{2,1,0:T(4,128)(2,1)}) %all-gather.5.cloned.1.call-update) | async-done | bytes 1048592 | tf_op jit(solution)/shard_map/all_gather | solution.py:134
  61.1 19.7 %copy.155 = bf16[2,4,16,8192]{2,1,0,3:T(4,128)(2,1)} copy(bf16[2,4,16,8192]{3,2,1,0:T(8,128)(2,1)} %select_multiply_fusion) | data formatting | bytes 4194304 | tf_op jit(solution)/shard_map/mul | solution.py:111
  80.7 20.8 %reshape.530 = bf16[16,2,32768]{2,1,0:T(2,128)(2,1)} reshape(bf16[8192,2,4,16]{3,2,1,0:T(4,128)(2,1)} %bitcast.134) | data formatting | bytes 4194304
  101.6 6.2 %all-to-all-start = ((bf16[16,2,32768]{2,1,0:T(2,128)(2,1)}), bf16[16,2,32768]{2,1,0:T(2,128)(2,1)}, u32[]{:S(2)}, u32[]{:S(2)}) async-start(bf16[16,2,32768]{2,1,0:T(2,128)(2,1)} %reshape.530), calls=%async_computation | async-start | bytes 4194304 | tf_op jit(solution)/shard_map/all_to_all | solution.py:113
  108.3 4.9 fusion.88
  113.3 35.7 %all-to-all-done = bf16[16,2,32768]{2,1,0:T(2,128)(2,1)} async-done(((bf16[16,2,32768]{2,1,0:T(2,128)(2,1)}), bf16[16,2,32768]{2,1,0:T(2,128)(2,1)}, u32[]{:S(2)}, u32[]{:S(2)}) %all-to-all-start) | async-done | bytes 2097184 | tf_op jit(solution)/shard_map/all_to_all | solution.py:113
  148.9 16.5 %reshape.531 = bf16[8192,2,4,16]{3,2,1,0:T(4,128)(2,1)} reshape(bf16[16,2,32768]{2,1,0:T(2,128)(2,1)} %all-to-all-done) | data formatting | bytes 4194304
  165.5 22.7 %copy.185 = bf16[2,4,16,16,512]{4,2,1,0,3:T(8,128)(2,1)} copy(bf16[2,4,16,16,512]{2,1,0,4,3:T(4,128)(2,1)} %bitcast.135) | data formatting | bytes 4194304 | tf_op jit(solution)/shard_map/all_to_all | solution.py:113
  196.3 39.7 %psum.28 = bf16[64,16]{0,1:T(8,128)(2,1)S(1)} all-reduce(f32[64,16]{0,1:T(8,128)S(1)} %fusion), channel_id=1, replica_groups=mesh['groups'=2,'pool'=1,'tensor'=16] {'tensor'}, use_global_device_ids=true, to_apply=%region_6.7 | all-reduce | flops 1024 | bytes 6144 | tf_op jit(solution)/shard_map/psum | solution.py:143
  241.7 6.7 %all-to-all-done.1 = bf16[16,4,512]{2,1,0:T(4,128)(2,1)S(1)} async-done(((bf16[16,4,512]{2,1,0:T(4,128)(2,1)}), bf16[16,4,512]{2,1,0:T(4,128)(2,1)S(1)}, u32[]{:S(2)}, u32[]{:S(2)}) %all-to-all-start.1) | async-done | bytes 65568 | tf_op jit(solution)/shard_map/all_to_all | solution.py:151
  249.9 9.5 %all_to_all.140 = bf16[4,16,512]{2,0,1:T(4,128)(2,1)S(1)} all-to-all(bf16[4,16,512]{2,0,1:T(4,128)(2,1)S(1)} %copy.163), channel_id=1, replica_groups=mesh['groups'=2,'pool'=1,'tensor'=16] {'tensor'}, dimensions={1} | all-to-all | bytes 131072 | tf_op jit(solution)/shard_map/all_to_all | solution.py:169
  259.4 6.3 %fusion.89 = f32[64,8192]{1,0:T(8,128)} fusion(bf16[64,512]{1,0:T(8,128)(2,1)S(1)} %all_to_all.116, bf16[512,8192]{1,0:T(8,128)(2,1)} %param.13), kind=kOutput, calls=%fused_computation.184 | convolution fusion | flops 536870912 | bytes 10551296 | tf_op jit(solution)/shard_map/dot_general | solution.py:173
  267.5 31.0 %psum.29 = bf16[64,16]{0,1:T(8,128)(2,1)S(1)} all-reduce(f32[64,16]{0,1:T(8,128)S(1)} %fusion.1), channel_id=1, replica_groups=mesh['groups'=2,'pool'=1,'tensor'=16] {'tensor'}, use_global_device_ids=true, to_apply=%region_11.12 | all-reduce | flops 1024 | bytes 6144 | tf_op jit(solution)/shard_map/psum | solution.py:182
  304.8 7.1 %all-to-all-done.4 = f32[16,4,512]{2,1,0:T(4,128)S(1)} async-done(((f32[16,4,512]{2,1,0:T(4,128)}), f32[16,4,512]{2,1,0:T(4,128)S(1)}, u32[]{:S(2)}, u32[]{:S(2)}) %all-to-all-start.4) | async-done | bytes 131104 | tf_op jit(solution)/shard_map/all_to_all | solution.py:184
  311.9 49.8 %all-reduce.5.cloned.1.call-done = f32[64,8192]{1,0:T(8,128)} async-done(((f32[64,8192]{1,0:T(8,128)}), f32[64,8192]{1,0:T(8,128)}) %all-reduce.5.cloned.1.call-update) | async-done | bytes 2097168
  363.6 37.7 %all-gather.7.cloned.1.call-done = bf16[16,4,8192]{2,1,0:T(4,128)(2,1)} async-done(((bf16[1,4,8192]{2,1,0:T(4,128)(2,1)}), bf16[16,4,8192]{2,1,0:T(4,128)(2,1)}) %all-gather.7.cloned.1.call-update) | async-done | bytes 1048592 | tf_op jit(solution)/shard_map/all_gather | solution.py:134
  404.0 5.1 fusion.90
  410.2 32.1 %psum.30 = bf16[64,16]{0,1:T(8,128)(2,1)S(1)} all-reduce(f32[64,16]{0,1:T(8,128)S(1)} %fusion.2), channel_id=1, replica_groups=mesh['groups'=2,'pool'=1,'tensor'=16] {'tensor'}, use_global_device_ids=true, to_apply=%region_14.15 | all-reduce | flops 1024 | bytes 6144 | tf_op jit(solution)/shard_map/psum | solution.py:143
  456.0 6.6 %all-to-all-done.5 = bf16[16,4,512]{2,1,0:T(4,128)(2,1)S(1)} async-done(((bf16[16,4,512]{2,1,0:T(4,128)(2,1)}), bf16[16,4,512]{2,1,0:T(4,128)(2,1)S(1)}, u32[]{:S(2)}, u32[]{:S(2)}) %all-to-all-start.5) | async-done | bytes 65568 | tf_op jit(solution)/shard_map/all_to_all | solution.py:151
  464.5 9.5 %all_to_all.141 = bf16[4,16,512]{2,0,1:T(4,128)(2,1)S(1)} all-to-all(bf16[4,16,512]{2,0,1:T(4,128)(2,1)S(1)} %copy.176), channel_id=1, replica_groups=mesh['groups'=2,'pool'=1,'tensor'=16] {'tensor'}, dimensions={1} | all-to-all | bytes 131072 | tf_op jit(solution)/shard_map/all_to_all | solution.py:169
  474.0 6.3 %fusion.91 = f32[64,8192]{1,0:T(8,128)} fusion(bf16[64,512]{1,0:T(8,128)(2,1)S(1)} %all_to_all.127, bf16[512,8192]{1,0:T(8,128)(2,1)} %param.13), kind=kOutput, calls=%fused_computation.186 | convolution fusion | flops 536870912 | bytes 10551296 | tf_op jit(solution)/shard_map/dot_general | solution.py:173
  481.8 31.1 %psum.31 = bf16[64,16]{0,1:T(8,128)(2,1)S(1)} all-reduce(f32[64,16]{0,1:T(8,128)S(1)} %fusion.3), channel_id=1, replica_groups=mesh['groups'=2,'pool'=1,'tensor'=16] {'tensor'}, use_global_device_ids=true, to_apply=%region_21.22 | all-reduce | flops 1024 | bytes 6144 | tf_op jit(solution)/shard_map/psum | solution.py:182
  514.7 11.1 %all_to_all.142 = f32[16,4,512]{2,1,0:T(4,128)S(1)} all-to-all(f32[16,4,512]{2,1,0:T(4,128)S(1)} %copy.179), channel_id=1, replica_groups=mesh['groups'=2,'pool'=1,'tensor'=16] {'tensor'}, dimensions={0} | all-to-all | bytes 262144 | tf_op jit(solution)/shard_map/all_to_all | solution.py:184
  525.7 50.8 %all-reduce.7.cloned.1.call-done = f32[64,8192]{1,0:T(8,128)} async-done(((f32[64,8192]{1,0:T(8,128)}), f32[64,8192]{1,0:T(8,128)}) %all-reduce.7.cloned.1.call-update) | async-done | bytes 2097168
  (137 shorter events, 66.4 us)
Async XLA Ops:
  6.5 4.1 copy-start
  6.5 43.7 %all-gather.5.cloned.1.call-start = ((), (), s32[]{:S(2)}) async-start(), calls=%async_computation.9 | async-start | bytes 1114112 | tf_op jit(solution)/shard_map/all_gather | solution.py:134
  54.2 47.3 %all-to-all-start.2 = ((bf16[16,4,128]{2,1,0:T(4,128)(2,1)}), bf16[16,4,128]{2,1,0:T(4,128)(2,1)S(1)}, u32[]{:S(2)}, u32[]{:S(2)}) async-start(bf16[16,4,128]{2,1,0:T(4,128)(2,1)} %bitcast.17), calls=%async_computation.2 | async-start | bytes 32768 | tf_op jit(solution)/shard_map/all_to_all | solution.py:152
  101.5 6.3 %copy-start.9 = (s32[4]{0:T(128)S(1)}, s32[4]{0:T(128)}, u32[]{:S(2)}) copy-start(s32[4]{0:T(128)} %param.19) | copy-start | bytes 52
  101.5 6.5 %copy-start.7 = (s32[64]{0:T(128)S(1)}, s32[64]{0:T(128)}, u32[]{:S(2)}) copy-start(s32[64]{0:T(128)} %param.18) | copy-start | bytes 772
  101.5 6.5 %copy-start.8 = (s32[32]{0:T(128)S(1)}, s32[32]{0:T(128)}, u32[]{:S(2)}) copy-start(s32[32]{0:T(128)} %param.17) | copy-start | bytes 388
  101.5 6.6 %copy-start.6 = (bf16[4,48,8,256]{3,2,1,0:T(8,128)(2,1)S(1)}, bf16[4,48,8,256]{3,2,1,0:T(8,128)(2,1)}, u32[]{:S(2)}) copy-start(bf16[4,48,8,256]{3,2,1,0:T(8,128)(2,1)} %param.14) | copy-start | bytes 2359300
  101.6 47.4 %all-to-all-start = ((bf16[16,2,32768]{2,1,0:T(2,128)(2,1)}), bf16[16,2,32768]{2,1,0:T(2,128)(2,1)}, u32[]{:S(2)}, u32[]{:S(2)}) async-start(bf16[16,2,32768]{2,1,0:T(2,128)(2,1)} %reshape.530), calls=%async_computation | async-start | bytes 4194304 | tf_op jit(solution)/shard_map/all_to_all | solution.py:113
  194.7 1.4 copy-start.3
  238.0 10.4 %all-to-all-start.1 = ((bf16[16,4,512]{2,1,0:T(4,128)(2,1)}), bf16[16,4,512]{2,1,0:T(4,128)(2,1)S(1)}, u32[]{:S(2)}, u32[]{:S(2)}) async-start(bf16[16,4,512]{2,1,0:T(4,128)(2,1)} %all_to_all.109), calls=%async_computation.1 | async-start | bytes 131072 | tf_op jit(solution)/shard_map/all_to_all | solution.py:151
  241.5 120.2 %all-reduce.5.cloned.1.call-start = ((), (), s32[]{:S(2)}) async-start(), calls=%async_computation.11 | async-start | bytes 4194304
  265.7 1.6 copy-start.4
  265.7 37.9 %copy-start.10 = (u32[32]{0:T(128)S(1)}, u32[32]{0:T(128)}, u32[]{:S(2)}) copy-start(u32[32]{0:T(128)} %constant.100) | copy-start | bytes 388
  265.7 96.0 %copy-start.5 = (bf16[4,8192]{1,0:T(4,128)(2,1)S(1)}, bf16[4,8192]{1,0:T(4,128)(2,1)}, u32[]{:S(2)}) copy-start(bf16[4,8192]{1,0:T(4,128)(2,1)} %param.10) | copy-start | bytes 196612
  299.9 12.0 %all-to-all-start.4 = ((f32[16,4,512]{2,1,0:T(4,128)}), f32[16,4,512]{2,1,0:T(4,128)S(1)}, u32[]{:S(2)}, u32[]{:S(2)}) async-start(f32[16,4,512]{2,1,0:T(4,128)} %copy.167), calls=%async_computation.4 | async-start | bytes 262144 | tf_op jit(solution)/shard_map/all_to_all | solution.py:184
  303.4 97.9 %all-gather.7.cloned.1.call-start = ((), (), s32[]{:S(2)}) async-start(), calls=%async_computation.10 | async-start | bytes 1114112 | tf_op jit(solution)/shard_map/all_gather | solution.py:134
  404.0 5.1 copy-start.2
  442.3 10.0 %all-to-all-start.6 = ((bf16[16,4,128]{2,1,0:T(4,128)(2,1)}), bf16[16,4,128]{2,1,0:T(4,128)(2,1)S(1)}, u32[]{:S(2)}, u32[]{:S(2)}) async-start(bf16[16,4,128]{2,1,0:T(4,128)(2,1)} %bitcast.40), calls=%async_computation.6 | async-start | bytes 32768 | tf_op jit(solution)/shard_map/all_to_all | solution.py:152
  452.3 10.4 %all-to-all-start.5 = ((bf16[16,4,512]{2,1,0:T(4,128)(2,1)}), bf16[16,4,512]{2,1,0:T(4,128)(2,1)S(1)}, u32[]{:S(2)}, u32[]{:S(2)}) async-start(bf16[16,4,512]{2,1,0:T(4,128)(2,1)} %all_to_all.120), calls=%async_computation.5 | async-start | bytes 131072 | tf_op jit(solution)/shard_map/all_to_all | solution.py:151
  455.8 120.8 %all-reduce.7.cloned.1.call-start = ((), (), s32[]{:S(2)}) async-start(), calls=%async_computation.12 | async-start | bytes 4194304
  480.3 98.0 %copy-start.1 = (bf16[2,4,16,8192]{3,2,1,0:T(8,128)(2,1)S(1)}, bf16[2,4,16,8192]{3,2,1,0:T(8,128)(2,1)}, u32[]{:S(2)}) copy-start(bf16[2,4,16,8192]{3,2,1,0:T(8,128)(2,1)} %param.15) | copy-start | bytes 6291460
Sparse Core Ops, SparseCore 0:
  9.5 40.6 all-gather.4
  265.8 95.8 all-reduce.4
  364.1 37.1 all-gather.6
  480.4 96.0 all-reduce.6
where the time goes:
time: 589 us; the launch traced here: 585 us
  waiting for transfers between devices  236 us (40%)
  blocking collectives  164 us (28%)
  local copies, waits for them, and re-layouts  94.6 us (16%)
  matrix products  36.3 us (6%)
  starting transfers between devices  24.2 us (4%)
  other arithmetic  15.1 us (3%)
  between operations  14.3 us (2%)
    unnamed x6, waiting for transfers between devices  101 us
    all_gather x2, waiting for transfers between devices, on_device(): lax.all_gather(normalized_input, 'tensor', axis=0, tiled=True)  75.2 us
    psum x2, blocking collectives, on_device(): lax.psum(projected[:, query_cols + keyval_cols:], 'tensor')  71.8 us
    psum x2, blocking collectives, on_device(): reduced_output = lax.psum(partial_out, 'tensor').astype(jnp.bfloat16)  62.1 us
    unnamed x27, local copies, waits for them, and re-layouts  43.2 us
    all_to_all x1, waiting for transfers between devices, on_device(): lax.all_to_all(doubled, ('pool', 'tensor'), split_axis=3, concat_axis=0,...  35.7 us
    all_to_all x1, local copies, waits for them, and re-layouts, on_device(): lax.all_to_all(doubled, ('pool', 'tensor'), split_axis=3, concat_axis=0,...  22.7 us
    mul x1, local copies, waits for them, and re-layouts, on_device(): jnp.take(adapter_pool, send_slots, axis=0) * present[:, None, None, None]  19.7 us
  transfers between devices with their start and end apart: 10, of which 9 were waited for; matrix products, arithmetic and copies ran while one was open for 10% of the time, Pallas kernels for 0%

commit v1 on v0

--- a/solution.py
+++ b/solution.py
@@ -1,6 +1,8 @@
 import jax
 import jax.numpy as jnp
 from jax import lax
+from jax.experimental import pallas as pl
+from jax.experimental.pallas import tpu as pltpu
 from jax.sharding import PartitionSpec as P
 
 HEADS = 64
@@ -192,9 +194,408 @@
     return jnp.stack(updates)
 
 
+DEVS = 16
+OWN = 4
+QUARTER = 2048
+CHUNKS = 2
+LANES = QUARTER // CHUNKS
+KEYS = 1536
+BF = jnp.bfloat16
+F32 = jnp.float32
+
+
+def iota(shape, dim):
+    return lax.broadcasted_iota(jnp.int32, shape, dim)
+
+
+def dot(a, b):
+    return jnp.dot(a, b, preferred_element_type=F32)
+
+
+def dot_nt(a, b):
+    return lax.dot_general(a, b, (((1,), (1,)), ((), ())), preferred_element_type=F32)
+
+
+def fused(
+    x0, page_col, page_row, length_col, cosine, sine, wq_hbm, wkv_hbm, wo_hbm, cache_hbm, pool_hbm,
+    out,
+    wq, wkv, wo, aq, bo, bq, ao, kvbuf, bias, perm, perm_t, perm_q,
+    x_cur, xs, xp, pb, bs, r1, s1, r2, s2, r3,
+    qs_send, qs_recv, tq, q_send, q_recv, a_send, a_recv, am, os_send, os_recv,
+    load_sem, ad_ss, ad_rs, agz_ss, agy_ss, agc_ss, ag_rs,
+    qs_ss, qs_rs, q_ss, q_rs, a_ss, a_rs, os_ss, os_rs,
+    rs1_ss, rs1_rs, rs2_ss, rs2_rs, rs3_ss, rs3_rs,
+):
+    me = lax.axis_index("tensor")
+    z, y, c = me // 4, (me // 2) % 2, me % 2
+    y_peer = z * 4 + (1 - y) * 2 + c
+    c_peer = z * 4 + y * 2 + (1 - c)
+
+    def remote(src, dst, ss, rs, peer):
+        return pltpu.make_async_remote_copy(
+            src_ref=src, dst_ref=dst, send_sem=ss, recv_sem=rs,
+            device_id={"tensor": peer}, device_id_type=pl.DeviceIdType.MESH,
+        )
+
+    def peers(body):
+        def one(i, carry):
+            body(lax.rem(me + i, DEVS))
+            return carry
+        lax.fori_loop(1, DEVS, one, 0)
+
+    loads = [
+        pltpu.make_async_copy(pool_hbm.at[:, 0], aq, load_sem.at[0]),
+        pltpu.make_async_copy(wq_hbm, wq, load_sem.at[1]),
+        pltpu.make_async_copy(wkv_hbm, wkv, load_sem.at[2]),
+        pltpu.make_async_copy(cache_hbm, kvbuf.at[pl.ds(0, KEYS)], load_sem.at[3]),
+        pltpu.make_async_copy(wo_hbm, wo, load_sem.at[4]),
+        pltpu.make_async_copy(pool_hbm.at[:, 3], bo, load_sem.at[5]),
+        pltpu.make_async_copy(
+            pool_hbm.at[:, 1, :, pl.ds(pl.multiple_of(me * 512, 512), 512)],
+            bq.at[pl.ds(2 * me, 2)], load_sem.at[6]),
+        pltpu.make_async_copy(
+            pool_hbm.at[:, 2, :, pl.ds(pl.multiple_of(me * 512, 512), 512)],
+            ao.at[pl.ds(2 * me, 2)], load_sem.at[7]),
+    ]
+    for load in loads:
+        load.start()
+
+    barrier = pltpu.get_barrier_semaphore()
+    peers(lambda d: pl.semaphore_signal(
+        barrier, inc=1, device_id={"tensor": d}, device_id_type=pl.DeviceIdType.MESH))
+    pl.semaphore_wait(barrier, DEVS - 1)
+
+    def ag_z(j, dz):
+        zz = lax.rem(z + dz, 4)
+        return remote(xs.at[j, me], xs.at[j, me], agz_ss.at[j, dz], ag_rs.at[j, me], zz * 4 + y * 2 + c)
+
+    def ag_y(j, zz):
+        b = zz * 4 + y * 2 + c
+        return remote(xs.at[j, b], xs.at[j, b], agy_ss.at[j, zz], ag_rs.at[j, b], y_peer)
+
+    def ag_c(j, zz, yy):
+        b = zz * 4 + yy * 2 + c
+        return remote(xs.at[j, b], xs.at[j, b], agc_ss.at[j, zz * 2 + yy], ag_rs.at[j, b], c_peer)
+
+    def ag_wait(j, b):
+        remote(xs.at[j, b], xs.at[j, b], agz_ss.at[j, 0], ag_rs.at[j, b], c_peer).wait_recv()
+
+    def ag_begin(j):
+        xs[j, me] = x_cur[j]
+        for dz in (1, 2, 3):
+            ag_z(j, dz).start()
+        ag_y(j, z).start()
+        ag_c(j, z, y).start()
+
+    def ag_forward(j):
+        for dz in (1, 2, 3):
+            zz = lax.rem(z + dz, 4)
+            ag_wait(j, zz * 4 + y * 2 + c)
+            ag_y(j, zz).start()
+            ag_c(j, zz, y).start()
+        for dz in range(4):
+            zz = lax.rem(z + dz, 4)
+            ag_wait(j, zz * 4 + (1 - y) * 2 + c)
+            ag_c(j, zz, 1 - y).start()
+
+    def ag_finish(j):
+        for b in range(8):
+            ag_wait(j, b * 2 + (1 - c))
+
+    def ag_drain(j):
+        for dz in (1, 2, 3):
+            ag_z(j, dz).wait_send()
+        for zz in range(4):
+            ag_y(j, zz).wait_send()
+            for yy in range(2):
+                ag_c(j, zz, yy).wait_send()
+
+    def adapter(kind, dst, d):
+        return remote(
+            pool_hbm.at[:, 1 + kind, :, pl.ds(pl.multiple_of(d * 512, 512), 512)],
+            dst.at[pl.ds(2 * me, 2)], ad_ss.at[kind, d], ad_rs.at[kind, me], d)
+
+    def adapter_wait(kind, dst):
+        loads[6 + kind].wait()
+
+        def one(d):
+            remote(
+                pool_hbm.at[:, 1 + kind, :, pl.ds(0, 512)],
+                dst.at[pl.ds(2 * d, 2)], ad_ss.at[kind, d], ad_rs.at[kind, d], d).wait_recv()
+        peers(one)
+
+    def spray(send, recv, ss, rs, per_peer):
+        def one(d):
+            src = send.at[d] if per_peer else send
+            remote(src, recv.at[me], ss.at[d], rs.at[me], d).start()
+        peers(one)
+
+    def spray_wait(send, recv, ss, rs, per_peer):
+        def one(d):
+            src = send.at[d] if per_peer else send
+            remote(src, recv.at[d], ss.at[d], rs.at[d], d).wait_recv()
+        peers(one)
+
+    def spray_drain(send, recv, ss, rs, per_peer):
+        def one(d):
+            src = send.at[d] if per_peer else send
+            remote(src, recv.at[me], ss.at[d], rs.at[me], d).wait_send()
+        peers(one)
+
+    for j in range(CHUNKS):
+        x_cur[j] = x0[j]
+        ag_begin(j)
+    peers(lambda d: adapter(0, bq, d).start())
+
+    i, k = iota((256, 256), 0), iota((256, 256), 1)
+    perm[...] = (k == ((i >> 2) & 15) * 16 + (i >> 6) * 4 + (i & 3)).astype(F32).astype(BF)
+    perm_t[...] = (k == ((i >> 2) & 3) * 64 + (i >> 4) * 4 + (i & 3)).astype(F32).astype(BF)
+    i, k = iota((512, 320), 0), iota((512, 320), 1)
+    perm_q[...] = (k == ((i >> 2) & 7) * 64 + (i >> 5) * 4 + (i & 3)).astype(F32).astype(BF)
+    qs_send[...] = jnp.zeros_like(qs_send)
+    os_send[...] = jnp.zeros_like(os_send)
+    kvbuf[pl.ds(KEYS, 256), :] = jnp.zeros((256, 256), BF)
+    for part in range(4):
+        keys = 384
+        i, k = iota((256, keys), 0), iota((256, keys), 1)
+        ok = ((i & 3) == part) & ((i >> 5) == (k & 7)) & ((k >> 3) < length_col[...])
+        bias[:, pl.ds(part * keys, keys)] = jnp.where(ok, 0.0, -1e30)
+    i, k = iota((256, 256), 0), iota((256, 256), 1)
+    fresh = ((k & 15) == (i & 3)) & (((k >> 4) & 7) == (i >> 5))
+    bias[:, pl.ds(KEYS, 256)] = jnp.where(fresh & (k < 128), 0.0, -1e30)
+
+    for j in range(CHUNKS):
+        ag_forward(j)
+    peers(lambda d: adapter(1, ao, d).start())
+    loads[0].wait()
+    loads[3].wait()
+
+    def step(s, carry):
+        @pl.when(s == 1)
+        def _():
+            i, k = iota((256, 256), 0), iota((256, 256), 1)
+            fresh = ((k & 15) == (i & 3)) & (((k >> 4) & 7) == (i >> 5))
+            bias[:, pl.ds(KEYS, 256)] = jnp.where(fresh, 0.0, -1e30)
+            for j in range(CHUNKS):
+                ag_forward(j)
+
+        squares = jnp.zeros((64, 1), F32)
+        shrink = jnp.zeros((32, 64), F32)
+        for j in range(CHUNKS):
+            ag_finish(j)
+            xp[j] = dot(perm[...], xs[j].reshape(256, LANES)).astype(BF)
+            for q in range(4):
+                x = xp[j, q * 64:(q + 1) * 64, :]
+                wide = x.astype(F32)
+                squares += jnp.sum(wide * wide, axis=1, keepdims=True)
+                a = aq[:, :, q * QUARTER + j * LANES:q * QUARTER + (j + 1) * LANES].reshape(32, LANES)
+                shrink += dot_nt(a, x)
+        here = page_row[...] == 2 * me + (iota((32, 64), 0) >> 4)
+        shrink = jnp.where(here, shrink, 0.0)
+        qs_send[:, 0:64] = (shrink[0:16] + shrink[16:32]).astype(BF)
+        qs_recv[me] = qs_send[...]
+        spray(qs_send, qs_recv, qs_ss, qs_rs, False)
+        scale = lax.rsqrt(squares * (1.0 / 8192.0) + norm_epsilon)
+
+        @pl.when(s == 0)
+        def _():
+            loads[1].wait()
+            loads[2].wait()
+
+        def project(n, acc):
+            j, q = n // 4, n % 4
+            x = xp[j, pl.ds(pl.multiple_of(q * 64, 64), 64), :]
+            at = pl.ds(pl.multiple_of(q * QUARTER + j * LANES, LANES), LANES)
+            return acc[0] + dot(x, wq[at, :]), acc[1] + dot(x, wkv[at, :])
+        query, keyval = lax.fori_loop(
+            0, 4 * CHUNKS, project, (jnp.zeros((64, 512), F32), jnp.zeros((64, 128), F32)))
+        tq[pl.ds(256, 64), :] = (keyval * scale).astype(BF)
+
+        spread_of = (iota((16, 512), 1) & 15) == iota((16, 512), 0)
+        spread_of = spread_of.astype(F32).astype(BF)
+        page_hit = page_col[...] == (iota((64, 512), 1) >> 4)
+
+        @pl.when(s == 0)
+        def _():
+            adapter_wait(0, bq)
+        spray_wait(qs_send, qs_recv, qs_ss, qs_rs, False)
+        qs = jnp.sum(qs_recv[...].astype(F32), axis=0)
+        low = dot(qs.T[0:64].astype(BF), spread_of)
+        low = jnp.where(page_hit, low, 0.0).astype(BF)
+        query = ((query + dot(low, bq[...].reshape(512, 512))) * scale).astype(BF)
+        for h in range(4):
+            tq[pl.ds(h * 64, 64), :] = query[:, h * 128:(h + 1) * 128]
+        q_send[...] = dot(perm_q[...], tq[...]).astype(BF).reshape(16, 32, 128)
+        q_recv[me] = q_send[me]
+        spray(q_send, q_recv, q_ss, q_rs, True)
+        spray_wait(q_send, q_recv, q_ss, q_rs, True)
+
+        cos, sin = cosine[s], sine[s]
+
+        def turn(v, n):
+            flat = v.astype(F32).reshape(n * 16, 128)
+            swapped = pltpu.roll(flat, 64, 1)
+            both = flat.reshape(n, 16, 128) * cos[None] + swapped.reshape(n, 16, 128) * sin[None]
+            return both.reshape(n * 16, 128).astype(BF)
+        queries = turn(q_recv[:, 0:16, :], 16)
+        fresh_kv = q_recv[:, 16:32, :].reshape(8, 2, 16, 128)
+        new_at = pl.ds(pl.multiple_of(KEYS + 128 * s, 128), 128)
+        kvbuf[new_at, 0:128] = turn(fresh_kv[:, 0], 8)
+        kvbuf[new_at, 128:256] = fresh_kv[:, 1].reshape(128, 128)
+        for half in range(2):
+            rows = slice(half * 128, half * 128 + 128)
+            score = dot_nt(queries[rows], kvbuf[:, 0:128]) * (float(HD) ** -0.5) + bias[rows, :]
+            power = jnp.exp(score - jnp.max(score, axis=1, keepdims=True))
+            total = jnp.sum(power, axis=1, keepdims=True)
+            mixed = dot(power.astype(BF), kvbuf[:, 128:256]) / total
+            a_send[half * 8:half * 8 + 8] = mixed.astype(BF).reshape(8, 16, 128)
+        a_recv[me] = a_send[me]
+        spray(a_send, a_recv, a_ss, a_rs, True)
+
+        @pl.when(s == 0)
+        def _():
+            adapter_wait(1, ao)
+            loads[4].wait()
+            loads[5].wait()
+        spray_wait(a_send, a_recv, a_ss, a_rs, True)
+
+        heads = dot(perm[...], a_recv[...].reshape(256, 128)).astype(BF)
+        for h in range(4):
+            am[:, h * 128:(h + 1) * 128] = heads[h * 64:(h + 1) * 64]
+        shrunk = dot_nt(ao[...].reshape(512, 512), am[...])
+        shrunk = jnp.where(page_row[...] == (iota((512, 64), 0) >> 4), shrunk, 0.0)
+        os_send[:, 0:64] = jnp.sum(shrunk.reshape(32, 16, 64), axis=0).astype(BF)
+        os_recv[me] = os_send[...]
+        spray(os_send, os_recv, os_ss, os_rs, False)
+
+        def low_out():
+            spray_wait(os_send, os_recv, os_ss, os_rs, False)
+            os = jnp.sum(os_recv[...].astype(F32), axis=0)
+            own = dot(os.T[0:64].astype(BF), spread_of[:, 0:32])
+            mine = page_col[...] == 2 * me + (iota((64, 32), 1) >> 4)
+            return jnp.where(mine, own, 0.0).astype(BF)
+
+        def rs1(j):
+            return remote(bs.at[j, :, 1 - c], r1.at[j], rs1_ss.at[j], rs1_rs.at[j], c_peer)
+
+        def rs2(j):
+            return remote(s1.at[j, :, 1 - y], r2.at[j], rs2_ss.at[j], rs2_rs.at[j], y_peer)
+
+        def rs3(j, dz):
+            zz = lax.rem(z + dz, 4)
+            return remote(s2.at[j, zz], r3.at[j, z], rs3_ss.at[j, dz], rs3_rs.at[j, z], zz * 4 + y * 2 + c)
+
+        def rs3_wait(j, zz):
+            remote(s2.at[j, zz], r3.at[j, zz], rs3_ss.at[j, 0], rs3_rs.at[j, zz], y_peer).wait_recv()
+
+        for j in range(CHUNKS):
+            ag_drain(j)
+        own = low_out()
+        for j in range(CHUNKS):
+            def outward(q, carry):
+                at = pl.ds(pl.multiple_of(q * QUARTER + j * LANES, LANES), LANES)
+                piece = dot(am[...], wo[:, at]) + dot(own, bo[:, :, at].reshape(32, LANES))
+                pb[pl.ds(pl.multiple_of(q * 64, 64), 64), :] = piece.astype(BF)
+                return carry
+            lax.fori_loop(0, 4, outward, 0)
+            bs[j] = dot(perm_t[...], pb[...]).astype(BF).reshape(8, 2, 16, LANES)
+            rs1(j).start()
+        for j in range(CHUNKS):
+            rs1(j).wait_recv()
+            s1[j] = (bs[j, :, c].astype(F32) + r1[j].astype(F32)).astype(BF).reshape(4, 2, 16, LANES)
+            rs2(j).start()
+        for j in range(CHUNKS):
+            rs2(j).wait_recv()
+            s2[j] = (s1[j, :, y].astype(F32) + r2[j].astype(F32)).astype(BF)
+            for dz in (1, 2, 3):
+                rs3(j, dz).start()
+        for j in range(CHUNKS):
+            total = s2[j, z].astype(F32)
+            for dz in (1, 2, 3):
+                zz = lax.rem(z + dz, 4)
+                rs3_wait(j, zz)
+                total += r3[j, zz].astype(F32)
+            update = total.astype(BF)
+            out[s, j] = update
+            x_cur[j] = (x_cur[j].astype(F32) + update.astype(F32)).astype(BF)
+
+            @pl.when(s == 0)
+            def _():
+                ag_begin(j)
+        for j in range(CHUNKS):
+            rs1(j).wait_send()
+            rs2(j).wait_send()
+            for dz in (1, 2, 3):
+                rs3(j, dz).wait_send()
+        spray_drain(qs_send, qs_recv, qs_ss, qs_rs, False)
+        spray_drain(q_send, q_recv, q_ss, q_rs, True)
+        spray_drain(a_send, a_recv, a_ss, a_rs, True)
+        spray_drain(os_send, os_recv, os_ss, os_rs, False)
+        return carry
+
+    lax.fori_loop(0, 2, step, 0)
+    peers(lambda d: adapter(0, bq, d).wait_send())
+    peers(lambda d: adapter(1, ao, d).wait_send())
+
+
+def on_device_fused(
+    hidden_state, query_weight, keyval_weight, output_weight, cache_entries, adapter_pool,
+    page_table, fetch_list, row_tenant, cache_length,
+):
+    tenants = jnp.arange(page_table.shape[0], dtype=jnp.int32)
+    row_page = jnp.sum(jnp.where(row_tenant[:, None] == tenants[None, :], page_table[None, :], 0), axis=1)
+    x0 = hidden_state.reshape(OWN, 4, CHUNKS, LANES).transpose(2, 1, 0, 3).reshape(CHUNKS, 16, LANES)
+    half = HD // 2
+    frequency = rope_base ** (-2.0 * jnp.arange(half, dtype=F32) / HD)
+    positions = cache_length[None, :] + jnp.arange(2, dtype=jnp.int32)[:, None]
+    angles = positions.astype(F32)[:, :, None] * frequency[None, None, :]
+    cos, sin = jnp.cos(angles), jnp.sin(angles)
+    cosine = jnp.tile(jnp.concatenate([cos, cos], axis=-1), (1, 4, 1))
+    sine = jnp.tile(jnp.concatenate([-sin, sin], axis=-1), (1, 4, 1))
+    length_col = jnp.tile(cache_length, 64)[:, None]
+    vmem = pl.BlockSpec(memory_space=pltpu.VMEM)
+    anywhere = pl.BlockSpec(memory_space=pl.ANY)
+    V = pltpu.VMEM
+    D_ = pltpu.SemaphoreType.DMA
+    result = pl.pallas_call(
+        fused,
+        out_shape=jax.ShapeDtypeStruct((2, CHUNKS, 16, LANES), BF),
+        in_specs=[vmem] * 6 + [anywhere] * 5,
+        out_specs=vmem,
+        scratch_shapes=[
+            V((8192, 512), BF), V((8192, 128), BF), V((512, 8192), BF),
+            V((2, 16, 8192), BF), V((2, 16, 8192), BF), V((32, 16, 512), BF), V((32, 16, 512), BF),
+            V((KEYS + 256, 256), BF), V((256, KEYS + 256), F32),
+            V((256, 256), BF), V((256, 256), BF), V((512, 320), BF),
+            V((CHUNKS, 16, LANES), BF), V((CHUNKS, 16, 16, LANES), BF), V((CHUNKS, 256, LANES), BF),
+            V((256, LANES), BF), V((CHUNKS, 8, 2, 16, LANES), BF),
+            V((CHUNKS, 8, 16, LANES), BF), V((CHUNKS, 4, 2, 16, LANES), BF),
+            V((CHUNKS, 4, 16, LANES), BF), V((CHUNKS, 4, 16, LANES), BF), V((CHUNKS, 4, 16, LANES), BF),
+            V((16, 128), BF), V((16, 16, 128), BF), V((320, 128), BF),
+            V((16, 32, 128), BF), V((16, 32, 128), BF),
+            V((16, 16, 128), BF), V((16, 16, 128), BF), V((64, 512), BF),
+            V((16, 128), BF), V((16, 16, 128), BF),
+            D_((8,)), D_((2, 16)), D_((2, 16)), D_((CHUNKS, 4)), D_((CHUNKS, 4)), D_((CHUNKS, 8)),
+            D_((CHUNKS, 16)),
+            D_((16,)), D_((16,)), D_((16,)), D_((16,)), D_((16,)), D_((16,)), D_((16,)), D_((16,)),
+            D_((CHUNKS,)), D_((CHUNKS,)), D_((CHUNKS,)), D_((CHUNKS,)), D_((CHUNKS, 4)), D_((CHUNKS, 4)),
+        ],
+        compiler_params=pltpu.CompilerParams(
+            collective_id=0, has_side_effects=True, vmem_limit_bytes=56 * 1024 * 1024),
+    )(
+        x0, row_page[:, None], row_page[None, :], length_col, cosine, sine,
+        query_weight, keyval_weight, output_weight, cache_entries.reshape(KEYS, 2 * HD), adapter_pool,
+    )
+    result = result.reshape(2, CHUNKS, 4, OWN, LANES).transpose(0, 3, 2, 1, 4)
+    return result.reshape(2, OWN, 4 * QUARTER)
+
+
 def solution(mesh):
+    local = on_device
+    if mesh.shape["tensor"] == DEVS and mesh.shape["pool"] == 1:
+        local = on_device_fused
     return jax.shard_map(
-        on_device,
+        local,
         mesh=mesh,
         in_specs=(
             P(("groups", "pool", "tensor"), None),

time: 589 us -> 132 us (0.22)
  waiting for transfers between devices: 236 us -> 0 us
  blocking collectives: 164 us -> 0 us
  Pallas kernels: 0 us -> 123 us
  local copies, waits for them, and re-layouts: 94.6 us -> 6.78 us
  matrix products: 36.3 us -> 0 us
  starting transfers between devices: 24.2 us -> 0 us
  between operations: 14.3 us -> 0.04 us
  other arithmetic: 15.1 us -> 1.63 us
    psum x4 -> x0, blocking collectives: 134 us -> none  [the longest x2 71.8 us: on_device(): lax.psum(projected[:, query_cols + keyval_cols:], 'tensor')]
    pallas_call x0 -> x1, Pallas kernels: none -> 123 us  [on_device_fused(): pl.pallas_call(fused, out_shape=jax.ShapeDtypeStruct((2, CHUNKS, 16, LANE...]
    unnamed x6 -> x0, waiting for transfers between devices: 101 us -> none
    all_gather x2 -> x0, waiting for transfers between devices: 75.2 us -> none  [on_device(): lax.all_gather(normalized_input, 'tensor', axis=0, tiled=True)]
    all_to_all x6 -> x0, waiting for transfers between devices: 60.6 us -> none  [the longest x1 35.7 us: on_device(): lax.all_to_all(doubled, ('pool', 'tensor'), split_axis=3, concat_axis=0,...]
    unnamed x27 -> x2, local copies, waits for them, and re-layouts: 43.2 us -> 0.01 us
    dot_general x21 -> x0, matrix products: 36.3 us -> none  [the longest x2 12.6 us: on_device(): jnp.dot(head_rows, output_weight, preferred_element_type=jnp.float32)]
    all_to_all x3 -> x0, blocking collectives: 30 us -> none  [the longest x2 19 us: on_device(): lax.all_to_all(attention_result, 'tensor', split_axis=1, concat_axis=0, t...]
  transfers between devices with their start and end apart: 10 -> 0, of which waited for: 9 -> 0; matrix products, arithmetic and copies ran while one was open for 10% -> 0% of each run, Pallas kernels for 0% -> 0%
where the time goes in v1:
time: 132 us
  Pallas kernels  123 us (93%)
  local copies, waits for them, and re-layouts  6.78 us (5%)
  other arithmetic  1.63 us (1%)
    pallas_call x1, Pallas kernels, on_device_fused(): pl.pallas_call(fused, out_shape=jax.ShapeDtypeStruct((2, CHUNKS, 16, LANE...  123 us

profile of v1, /device:TPU:0, one launch (start us, length us, event | category | flops | bytes accessed | tf_op | source)
XLA Modules:
  0.0 131.9 jit_solution(15613531720129446184)
XLA Ops:
  0.0 0.8 select_reduce_fusion
  0.8 0.0 copy-start
  0.8 0.7 add_convert_fusion
  1.4 0.1 fusion
  1.6 0.1 pad_maximum_fusion
  1.6 0.6 tile.11
  2.2 0.6 tile.13
  2.8 0.7 copy.18.page_col
  3.6 0.7 tile.10
  4.2 0.9 reshape.48
  5.1 0.1 copy.22
  5.2 0.7 reshape.49.x0
  5.8 0.7 broadcast_in_dim_tile.4.length_col
  6.6 0.0 copy-done
  6.6 123.4 %shard_map.91 = bf16[2,2,16,1024]{3,2,1,0:T(8,128)(2,1)} custom-call(bf16[2,16,1024]{2,1,0:T(8,128)(2,1)} %reshape.49.x0, s32[64,1]{1,0:T(8,128)} %copy.18.page_col, s32[1,64]{1,0:T(1,128)} %bitcast.17, s32[256,1]{1,0:T(8,128)} %broadcast_in_dim_tile.4.length_col, f32[2,16,128]{2,1,0:T(8,128)} %bitcast.14, f32[2,16,128]{2,1,0:T(8,128)} %bitcast.15, ...), custom_call_target="tpu_custom_call" | custom-call | tf_op jit(solution)/shard_map/pallas_call | solution.py:560
  130.0 1.0 reshape.51
  131.0 0.1 copy.20
  131.1 0.7 reshape.52
  (1 shorter events, 0.0 us)
Async XLA Ops:
  0.8 5.8 %copy-start = (s32[64]{0:T(128)}, s32[64]{0:T(128)S(1)}, u32[]{:S(2)}) copy-start(s32[64]{0:T(128)S(1)} %select_reduce_fusion) | copy-start | bytes 772

commit v2 on v1

--- a/solution.py
+++ b/solution.py
@@ -1,3 +1,5 @@
+import math
+
 import jax
 import jax.numpy as jnp
 from jax import lax
@@ -217,10 +219,10 @@
 
 
 def fused(
-    x0, page_col, page_row, length_col, cosine, sine, wq_hbm, wkv_hbm, wo_hbm, cache_hbm, pool_hbm,
+    x0, page_table, row_tenant, cache_length, wq_hbm, wkv_hbm, wo_hbm, cache_hbm, pool_hbm,
     out,
     wq, wkv, wo, aq, bo, bq, ao, kvbuf, bias, perm, perm_t, perm_q,
-    x_cur, xs, xp, pb, bs, r1, s1, r2, s2, r3,
+    page_col, page_row, cosine, sine, x_cur, xs, xp, pw, pb, bs, r1, s1, r2, s2, r3,
     qs_send, qs_recv, tq, q_send, q_recv, a_send, a_recv, am, os_send, os_recv,
     load_sem, ad_ss, ad_rs, agz_ss, agy_ss, agc_ss, ag_rs,
     qs_ss, qs_rs, q_ss, q_rs, a_ss, a_rs, os_ss, os_rs,
@@ -238,10 +240,8 @@
         )
 
     def peers(body):
-        def one(i, carry):
+        for i in range(1, DEVS):
             body(lax.rem(me + i, DEVS))
-            return carry
-        lax.fori_loop(1, DEVS, one, 0)
 
     loads = [
         pltpu.make_async_copy(pool_hbm.at[:, 0], aq, load_sem.at[0]),
@@ -293,6 +293,8 @@
             ag_wait(j, zz * 4 + y * 2 + c)
             ag_y(j, zz).start()
             ag_c(j, zz, y).start()
+
+    def ag_cross(j):
         for dz in range(4):
             zz = lax.rem(z + dz, 4)
             ag_wait(j, zz * 4 + (1 - y) * 2 + c)
@@ -343,9 +345,34 @@
         peers(one)
 
     for j in range(CHUNKS):
-        x_cur[j] = x0[j]
+        x_cur[j] = jnp.concatenate(
+            [x0[:, q * QUARTER + j * LANES:q * QUARTER + (j + 1) * LANES].astype(F32) for q in range(4)],
+            axis=0).astype(BF)
         ag_begin(j)
     peers(lambda d: adapter(0, bq, d).start())
+    peers(lambda d: adapter(1, ao, d).start())
+
+    col, line = jnp.zeros((64, 128), jnp.int32), jnp.zeros((8, 64), jnp.int32)
+    for r in range(64):
+        page = page_table[row_tenant[r]]
+        col = jnp.where(iota((64, 128), 0) == r, page, col)
+        line = jnp.where(iota((8, 64), 1) == r, page, line)
+    for n in range(4):
+        page_col[:, n * 128:(n + 1) * 128] = col
+    page_row[...] = line
+
+    def by_row(shape):
+        got = jnp.zeros(shape, jnp.int32)
+        for r in range(OWN):
+            got = jnp.where((iota(shape, 0) & 3) == r, cache_length[r], got)
+        return got
+    lane = iota((16, 128), 1)
+    frequency = jnp.exp((lane & 63).astype(F32) * (-2.0 / HD * math.log(rope_base)))
+    for n in range(2):
+        angle = (by_row((16, 128)) + n).astype(F32) * frequency
+        cosine[n] = jnp.cos(angle)
+        turned = jnp.sin(angle)
+        sine[n] = jnp.where(lane < 64, -turned, turned)
 
     i, k = iota((256, 256), 0), iota((256, 256), 1)
     perm[...] = (k == ((i >> 2) & 15) * 16 + (i >> 6) * 4 + (i & 3)).astype(F32).astype(BF)
@@ -358,7 +385,7 @@
     for part in range(4):
         keys = 384
         i, k = iota((256, keys), 0), iota((256, keys), 1)
-        ok = ((i & 3) == part) & ((i >> 5) == (k & 7)) & ((k >> 3) < length_col[...])
+        ok = ((i & 3) == part) & ((i >> 5) == (k & 7)) & ((k >> 3) < by_row((256, keys)))
         bias[:, pl.ds(part * keys, keys)] = jnp.where(ok, 0.0, -1e30)
     i, k = iota((256, 256), 0), iota((256, 256), 1)
     fresh = ((k & 15) == (i & 3)) & (((k >> 4) & 7) == (i >> 5))
@@ -366,7 +393,8 @@
 
     for j in range(CHUNKS):
         ag_forward(j)
-    peers(lambda d: adapter(1, ao, d).start())
+    for j in range(CHUNKS):
+        ag_cross(j)
     loads[0].wait()
     loads[3].wait()
 
@@ -378,6 +406,8 @@
             bias[:, pl.ds(KEYS, 256)] = jnp.where(fresh, 0.0, -1e30)
             for j in range(CHUNKS):
                 ag_forward(j)
+            for j in range(CHUNKS):
+                ag_cross(j)
 
         squares = jnp.zeros((64, 1), F32)
         shrink = jnp.zeros((32, 64), F32)
@@ -390,7 +420,7 @@
                 squares += jnp.sum(wide * wide, axis=1, keepdims=True)
                 a = aq[:, :, q * QUARTER + j * LANES:q * QUARTER + (j + 1) * LANES].reshape(32, LANES)
                 shrink += dot_nt(a, x)
-        here = page_row[...] == 2 * me + (iota((32, 64), 0) >> 4)
+        here = page_row[0:1, :] == 2 * me + (iota((32, 64), 0) >> 4)
         shrink = jnp.where(here, shrink, 0.0)
         qs_send[:, 0:64] = (shrink[0:16] + shrink[16:32]).astype(BF)
         qs_recv[me] = qs_send[...]
@@ -463,7 +493,7 @@
         for h in range(4):
             am[:, h * 128:(h + 1) * 128] = heads[h * 64:(h + 1) * 64]
         shrunk = dot_nt(ao[...].reshape(512, 512), am[...])
-        shrunk = jnp.where(page_row[...] == (iota((512, 64), 0) >> 4), shrunk, 0.0)
+        shrunk = jnp.where(page_row[0:1, :] == (iota((512, 64), 0) >> 4), shrunk, 0.0)
         os_send[:, 0:64] = jnp.sum(shrunk.reshape(32, 16, 64), axis=0).astype(BF)
         os_recv[me] = os_send[...]
         spray(os_send, os_recv, os_ss, os_rs, False)
@@ -472,7 +502,7 @@
             spray_wait(os_send, os_recv, os_ss, os_rs, False)
             os = jnp.sum(os_recv[...].astype(F32), axis=0)
             own = dot(os.T[0:64].astype(BF), spread_of[:, 0:32])
-            mine = page_col[...] == 2 * me + (iota((64, 32), 1) >> 4)
+            mine = page_col[:, 0:32] == 2 * me + (iota((64, 32), 1) >> 4)
             return jnp.where(mine, own, 0.0).astype(BF)
 
         def rs1(j):
@@ -490,14 +520,19 @@
 
         for j in range(CHUNKS):
             ag_drain(j)
+        def outward(n, carry):
+            j, q = n // 4, n % 4
+            at = pl.ds(pl.multiple_of(q * QUARTER + j * LANES, LANES), LANES)
+            pw[pl.ds(pl.multiple_of(n * 64, 64), 64), :] = dot(am[...], wo[:, at])
+            return carry
+        lax.fori_loop(0, 4 * CHUNKS, outward, 0)
         own = low_out()
         for j in range(CHUNKS):
-            def outward(q, carry):
-                at = pl.ds(pl.multiple_of(q * QUARTER + j * LANES, LANES), LANES)
-                piece = dot(am[...], wo[:, at]) + dot(own, bo[:, :, at].reshape(32, LANES))
-                pb[pl.ds(pl.multiple_of(q * 64, 64), 64), :] = piece.astype(BF)
-                return carry
-            lax.fori_loop(0, 4, outward, 0)
+            for q in range(4):
+                n = j * 4 + q
+                at = slice(q * QUARTER + j * LANES, q * QUARTER + (j + 1) * LANES)
+                piece = pw[n * 64:(n + 1) * 64, :] + dot(own, bo[:, :, at].reshape(32, LANES))
+                pb[q * 64:(q + 1) * 64, :] = piece.astype(BF)
             bs[j] = dot(perm_t[...], pb[...]).astype(BF).reshape(8, 2, 16, LANES)
             rs1(j).start()
         for j in range(CHUNKS):
@@ -542,33 +577,24 @@
     hidden_state, query_weight, keyval_weight, output_weight, cache_entries, adapter_pool,
     page_table, fetch_list, row_tenant, cache_length,
 ):
-    tenants = jnp.arange(page_table.shape[0], dtype=jnp.int32)
-    row_page = jnp.sum(jnp.where(row_tenant[:, None] == tenants[None, :], page_table[None, :], 0), axis=1)
-    x0 = hidden_state.reshape(OWN, 4, CHUNKS, LANES).transpose(2, 1, 0, 3).reshape(CHUNKS, 16, LANES)
-    half = HD // 2
-    frequency = rope_base ** (-2.0 * jnp.arange(half, dtype=F32) / HD)
-    positions = cache_length[None, :] + jnp.arange(2, dtype=jnp.int32)[:, None]
-    angles = positions.astype(F32)[:, :, None] * frequency[None, None, :]
-    cos, sin = jnp.cos(angles), jnp.sin(angles)
-    cosine = jnp.tile(jnp.concatenate([cos, cos], axis=-1), (1, 4, 1))
-    sine = jnp.tile(jnp.concatenate([-sin, sin], axis=-1), (1, 4, 1))
-    length_col = jnp.tile(cache_length, 64)[:, None]
     vmem = pl.BlockSpec(memory_space=pltpu.VMEM)
+    scalars = pl.BlockSpec(memory_space=pltpu.SMEM)
     anywhere = pl.BlockSpec(memory_space=pl.ANY)
     V = pltpu.VMEM
     D_ = pltpu.SemaphoreType.DMA
     result = pl.pallas_call(
         fused,
         out_shape=jax.ShapeDtypeStruct((2, CHUNKS, 16, LANES), BF),
-        in_specs=[vmem] * 6 + [anywhere] * 5,
+        in_specs=[vmem] + [scalars] * 3 + [anywhere] * 5,
         out_specs=vmem,
         scratch_shapes=[
             V((8192, 512), BF), V((8192, 128), BF), V((512, 8192), BF),
             V((2, 16, 8192), BF), V((2, 16, 8192), BF), V((32, 16, 512), BF), V((32, 16, 512), BF),
             V((KEYS + 256, 256), BF), V((256, KEYS + 256), F32),
             V((256, 256), BF), V((256, 256), BF), V((512, 320), BF),
+            V((64, 512), jnp.int32), V((8, 64), jnp.int32), V((2, 16, 128), F32), V((2, 16, 128), F32),
             V((CHUNKS, 16, LANES), BF), V((CHUNKS, 16, 16, LANES), BF), V((CHUNKS, 256, LANES), BF),
-            V((256, LANES), BF), V((CHUNKS, 8, 2, 16, LANES), BF),
+            V((CHUNKS * 256, LANES), F32), V((256, LANES), BF), V((CHUNKS, 8, 2, 16, LANES), BF),
             V((CHUNKS, 8, 16, LANES), BF), V((CHUNKS, 4, 2, 16, LANES), BF),
             V((CHUNKS, 4, 16, LANES), BF), V((CHUNKS, 4, 16, LANES), BF), V((CHUNKS, 4, 16, LANES), BF),
             V((16, 128), BF), V((16, 16, 128), BF), V((320, 128), BF),
@@ -583,7 +609,7 @@
         compiler_params=pltpu.CompilerParams(
             collective_id=0, has_side_effects=True, vmem_limit_bytes=56 * 1024 * 1024),
     )(
-        x0, row_page[:, None], row_page[None, :], length_col, cosine, sine,
+        hidden_state, page_table, row_tenant, cache_length,
         query_weight, keyval_weight, output_weight, cache_entries.reshape(KEYS, 2 * HD), adapter_pool,
     )
     result = result.reshape(2, CHUNKS, 4, OWN, LANES).transpose(0, 3, 2, 1, 4)

time: 132 us -> 118 us (0.89)
  Pallas kernels: 123 us -> 116 us
  local copies, waits for them, and re-layouts: 6.78 us -> 1.84 us
  other arithmetic: 1.63 us -> 0 us
    pallas_call x1, Pallas kernels: 123 us -> 116 us  [on_device_fused(): pl.pallas_call(fused, out_shape=jax.ShapeDtypeStruct((2, CHUNKS, 16, LANE...]
    another operation x4 -> x0, local copies, waits for them, and re-layouts: 2.61 us -> none  [the longest x2 1.4 us: on_device_fused(): length_col = jnp.tile(cache_length, 64)[:, None]]
    reshape x3 -> x0, local copies, waits for them, and re-layouts: 1.62 us -> none  [on_device_fused(): hidden_state.reshape(OWN, 4, CHUNKS, LANES).transpose(2, 1, 0, 3)]
where the time goes in v2:
time: 118 us
  Pallas kernels  116 us (98%)
  local copies, waits for them, and re-layouts  1.84 us (2%)
    pallas_call x1, Pallas kernels, on_device_fused(): pl.pallas_call(fused, out_shape=jax.ShapeDtypeStruct((2, CHUNKS, 16, LANE...  116 us

profile of v2, /device:TPU:0, one launch (start us, length us, event | category | flops | bytes accessed | tf_op | source)
XLA Modules:
  0.0 118.3 jit_solution(2128676038302798755)
XLA Ops:
  0.0 116.4 %shard_map.91 = bf16[2,2,16,1024]{3,2,1,0:T(8,128)(2,1)} custom-call(bf16[4,8192]{1,0:T(4,128)(2,1)} %x0.1, s32[32]{0:T(128)} %page_table.1, s32[64]{0:T(128)} %row_tenant.1, s32[4]{0:T(128)} %cache_length.1, bf16[8192,512]{1,0:T(8,128)(2,1)} %wq_hbm.1, bf16[8192,128]{1,0:T(8,128)(2,1)} %wkv_hbm.1, bf16[512,8192]{1,0:T(8,128)(2,1)} %wo_hbm.1, ...), custom_call_target="tpu_custom_call" | custom-call | tf_op jit(solution)/shard_map/pallas_call | solution.py:585
  116.4 1.0 reshape.10
  117.4 0.1 copy.10
  117.6 0.7 reshape.11

commit v3 on v2

--- a/solution.py
+++ b/solution.py
@@ -526,6 +526,14 @@
             pw[pl.ds(pl.multiple_of(n * 64, 64), 64), :] = dot(am[...], wo[:, at])
             return carry
         lax.fori_loop(0, 4 * CHUNKS, outward, 0)
+        spray_drain(qs_send, qs_recv, qs_ss, qs_rs, False)
+        spray_drain(q_send, q_recv, q_ss, q_rs, True)
+        spray_drain(a_send, a_recv, a_ss, a_rs, True)
+
+        @pl.when(s == 1)
+        def _():
+            peers(lambda d: adapter(0, bq, d).wait_send())
+            peers(lambda d: adapter(1, ao, d).wait_send())
         own = low_out()
         for j in range(CHUNKS):
             for q in range(4):
@@ -562,15 +570,10 @@
             rs2(j).wait_send()
             for dz in (1, 2, 3):
                 rs3(j, dz).wait_send()
-        spray_drain(qs_send, qs_recv, qs_ss, qs_rs, False)
-        spray_drain(q_send, q_recv, q_ss, q_rs, True)
-        spray_drain(a_send, a_recv, a_ss, a_rs, True)
         spray_drain(os_send, os_recv, os_ss, os_rs, False)
         return carry
 
     lax.fori_loop(0, 2, step, 0)
-    peers(lambda d: adapter(0, bq, d).wait_send())
-    peers(lambda d: adapter(1, ao, d).wait_send())
 
 
 def on_device_fused(

time: 118 us -> 118 us (level)
  no operation moved by 1% of the time
where the time goes in v3:
time: 118 us
  Pallas kernels  116 us (98%)
  local copies, waits for them, and re-layouts  1.84 us (2%)
    pallas_call x1, Pallas kernels, on_device_fused(): pl.pallas_call(fused, out_shape=jax.ShapeDtypeStruct((2, CHUNKS, 16, LANE...  116 us

profile of v3, /device:TPU:0, one launch (start us, length us, event | category | flops | bytes accessed | tf_op | source)
XLA Modules:
  0.0 118.2 jit_solution(17328415814453250301)
XLA Ops:
  0.0 116.3 %shard_map.91 = bf16[2,2,16,1024]{3,2,1,0:T(8,128)(2,1)} custom-call(bf16[4,8192]{1,0:T(4,128)(2,1)} %x0.1, s32[32]{0:T(128)} %page_table.1, s32[64]{0:T(128)} %row_tenant.1, s32[4]{0:T(128)} %cache_length.1, bf16[8192,512]{1,0:T(8,128)(2,1)} %wq_hbm.1, bf16[8192,128]{1,0:T(8,128)(2,1)} %wkv_hbm.1, bf16[512,8192]{1,0:T(8,128)(2,1)} %wo_hbm.1, ...), custom_call_target="tpu_custom_call" | custom-call | tf_op jit(solution)/shard_map/pallas_call | solution.py:588
  116.3 1.0 reshape.10
  117.3 0.1 copy.10
  117.4 0.7 reshape.11
